TPU v7x, 32 devices: a whole 2x2x4 slice. The times are simulated.
32 devices in a mesh: dp: 32 (over z, y, x, core).
Axes of the slice: x: 2, y: 2, z: 4, core: 2. Of those that a mesh axis runs over, the one named last changes fastest.
Arguments:
- frames: bfloat16 [256, 16, 16, 128], P('dp'), may hold values from -6 to 6
- clip_blocks: int32 [4], replicated, may hold values from 1 to 16, 32 in all
- tail_frames: int32 [4], replicated, may hold values from 1 to 8
- weight_one: bfloat16 [3, 3, 3, 128, 128], replicated, may hold values from -0.109375 to 0.109375
- weight_two: bfloat16 [3, 3, 3, 128, 256], replicated, may hold values from -0.109375 to 0.109375
- cotangent: bfloat16 [256, 16, 16, 256], P('dp'), may hold values from -6 to 6
Outputs:
- features: bfloat16 [256, 16, 16, 256], P('dp')
- grad_one: float32 [3, 3, 3, 128, 128], replicated
- grad_two: float32 [3, 3, 3, 128, 256], replicated
Inputs may be any that keep to these rules, and one draw needn't show every extreme that they name: `clip_blocks`: the blocks of all clips add up to 32; the longest clip has exactly 16 blocks.
All inputs are finite; a program needn't handle non-finite values.
Results may differ from a plain program's by a relative error of at most 0.005.
Values may be sent and summed in bfloat16 or wider, within the bound.
A program may use at most 64 MiB of HBM per device.

v0:
```python
import functools
import math

import jax
import jax.numpy as jnp
from jax import lax
from jax.experimental import pallas as pl
from jax.experimental.pallas import tpu as pltpu
from jax.sharding import PartitionSpec as P

LANES = 128


def bit_order(chunk, levels):
    middle = list(range(1, levels - 1))
    turn = chunk % max(1, len(middle))
    return [0] + middle[turn:] + middle[:turn] + [levels - 1]


def sum_kernel(levels, one_ref, two_ref, out_ref, acc, sent, came, rs_send, rs_recv, ag_send, ag_recv):
    chunks, rows = (acc.shape[0], acc.shape[1])
    real = one_ref.shape[0]
    me = lax.axis_index("dp")
    bits = [lax.rem(me // (1 << k), 2) for k in range(levels)]
    partners = [me + (1 - 2 * bits[k]) * (1 << k) for k in range(levels)]
    orders = [bit_order(chunk, levels) for chunk in range(chunks)]

    barrier = pltpu.get_barrier_semaphore()
    for k in range(levels):
        pl.semaphore_signal(barrier, inc=1, device_id=(partners[k],), device_id_type=pl.DeviceIdType.MESH)

    wide = one_ref.shape[1] // LANES
    for chunk in range(chunks):
        ref, col = (one_ref, chunk) if chunk < wide else (two_ref, chunk - wide)
        acc[chunk, :real, :] = ref[:, col * LANES : (col + 1) * LANES]
        if rows > real:
            acc[chunk, real:, :] = jnp.zeros((rows - real, LANES), jnp.float32)

    pl.semaphore_wait(barrier, levels)

    def aligned(value):
        return pl.multiple_of(value, 16)

    def scatter_copy(chunk, step):
        size = rows >> (step + 1)
        at = rows - (rows >> step)
        return pltpu.make_async_remote_copy(
            src_ref=sent.at[chunk, pl.ds(at, size)],
            dst_ref=came.at[chunk, pl.ds(at, size)],
            send_sem=rs_send.at[chunk, step],
            recv_sem=rs_recv.at[chunk, step],
            device_id=(partners[orders[chunk][step]],),
            device_id_type=pl.DeviceIdType.MESH,
        )

    def gather_copy(chunk, step, base):
        size = rows >> (step + 1)
        return pltpu.make_async_remote_copy(
            src_ref=out_ref.at[chunk, pl.ds(aligned(base), size)],
            dst_ref=out_ref.at[chunk, pl.ds(aligned(base), size)],
            send_sem=ag_send.at[chunk, step],
            recv_sem=ag_recv.at[chunk, step],
            device_id=(partners[orders[chunk][step]],),
            device_id_type=pl.DeviceIdType.MESH,
        )

    base = [jnp.int32(0)] * chunks
    copies = [None] * chunks
    pending = []

    def send_half(chunk, step):
        size = rows >> (step + 1)
        at = rows - (rows >> step)
        bit = bits[orders[chunk][step]]
        away = aligned(base[chunk] + (1 - bit) * size)
        sent[chunk, pl.ds(at, size), :] = acc[chunk, pl.ds(away, size), :].astype(jnp.bfloat16)
        copies[chunk] = scatter_copy(chunk, step)
        copies[chunk].start()
        pending.append(copies[chunk])
        base[chunk] = base[chunk] + bit * size

    for chunk in range(chunks):
        send_half(chunk, 0)
    for step in range(levels):
        size = rows >> (step + 1)
        at = rows - (rows >> step)
        for chunk in range(chunks):
            copies[chunk].wait_recv()
            here = pl.ds(aligned(base[chunk]), size)
            total = acc[chunk, here, :] + came[chunk, pl.ds(at, size), :].astype(jnp.float32)
            if step + 1 < levels:
                acc[chunk, here, :] = total
                send_half(chunk, step + 1)
            else:
                out_ref[chunk, here, :] = total.astype(jnp.bfloat16)
                copies[chunk] = gather_copy(chunk, step, base[chunk])
                copies[chunk].start()
                pending.append(copies[chunk])
    for step in reversed(range(levels)):
        size = rows >> (step + 1)
        for chunk in range(chunks):
            copies[chunk].wait_recv()
            base[chunk] = base[chunk] - bits[orders[chunk][step]] * size
            if step > 0:
                copies[chunk] = gather_copy(chunk, step - 1, base[chunk])
                copies[chunk].start()
                pending.append(copies[chunk])
    for copy in pending:
        copy.wait_send()


def sum_over_devices(one, two):
    devices = lax.axis_size("dp")
    levels = devices.bit_length() - 1
    assert devices == 1 << levels
    shape_one, shape_two = (one.shape, two.shape)
    one = one.reshape(-1, one.shape[-1])
    two = two.reshape(-1, two.shape[-1])
    real = one.shape[0]
    step = 16 * devices
    rows = -(-real // step) * step
    chunks = (one.shape[1] + two.shape[1]) // LANES
    summed = pl.pallas_call(
        functools.partial(sum_kernel, levels),
        out_shape=jax.ShapeDtypeStruct((chunks, rows, LANES), jnp.bfloat16),
        in_specs=[pl.BlockSpec(memory_space=pltpu.VMEM)] * 2,
        out_specs=pl.BlockSpec(memory_space=pltpu.VMEM),
        scratch_shapes=[
            pltpu.VMEM((chunks, rows, LANES), jnp.float32),
            pltpu.VMEM((chunks, rows, LANES), jnp.bfloat16),
            pltpu.VMEM((chunks, rows, LANES), jnp.bfloat16),
        ]
        + [pltpu.SemaphoreType.DMA((chunks, levels))] * 4,
        compiler_params=pltpu.CompilerParams(
            collective_id=0, has_side_effects=True, vmem_limit_bytes=40 * 1024 * 1024
        ),
    )(one, two)
    summed = summed[:, :real].astype(jnp.float32)
    wide = one.shape[1] // LANES
    whole = [summed[chunk] for chunk in range(chunks)]
    grad_one = jnp.concatenate(whole[:wide], axis=1).reshape(shape_one)
    grad_two = jnp.concatenate(whole[wide:], axis=1).reshape(shape_two)
    return grad_one, grad_two


def from_behind(value, axis, steps):
    count = lax.axis_size(axis)
    initial, last = (max(0, -steps), min(count, count - steps))
    return lax.ppermute(value, axis, [(source, source + steps) for source in range(initial, last)])


def spread(source, target, width):
    count, pixels, channels = source.shape
    column = lax.broadcasted_iota(jnp.int32, (pixels, channels), 0) % width

    @pl.loop(0, count)
    def _(f):
        value = source[f]
        wide = value.astype(jnp.float32)
        left = jnp.where(column == 0, 0.0, pltpu.roll(wide, 1, 0)).astype(jnp.bfloat16)
        right = jnp.where(column == width - 1, 0.0, pltpu.roll(wide, pixels - 1, 0)).astype(jnp.bfloat16)
        blank = jnp.zeros((width, channels), jnp.bfloat16)
        for kw, moved in enumerate((left, value, right)):
            target[f, :, (3 + kw) * channels : (4 + kw) * channels] = moved
            cols = slice(kw * channels, (kw + 1) * channels)
            target[f, width:, cols] = moved[: pixels - width]
            target[f, :width, cols] = blank
            cols = slice((6 + kw) * channels, (7 + kw) * channels)
            target[f, : pixels - width, cols] = moved[width:]
            target[f, pixels - width :, cols] = blank


def turn(taps, first, turned, channels):
    pixels = taps.shape[1]

    @pl.loop(0, turned.shape[1] // pixels)
    def _(f):
        at = pl.ds(pl.multiple_of(f * pixels, pixels), pixels)
        for tap in range(9):
            cols = slice(tap * channels, (tap + 1) * channels)
            turned[cols, at] = taps[first + f, :, cols].T


def outer(turned, grad, result, pixels):
    rows = grad.shape[0]
    height = turned.shape[0] // 3
    for kt in range(3):

        @pl.loop(0, 3)
        def _(kh):
            at = pl.ds(pl.multiple_of(kh * height, height), height)
            result[kt, at, :] = jnp.dot(
                turned[at, kt * pixels : kt * pixels + rows], grad[...], preferred_element_type=jnp.float32
            )


def back_kernel(width, scale, valid_ref, cot_ref, weight_ref, dout_ref, head_ref, tail_ref, taps, flipped, back):
    count, pixels, channels = cot_ref.shape
    inner = tail_ref.shape[2]
    valid = valid_ref[0]

    @pl.loop(0, count)
    def _(f):
        used = jnp.where(f < valid, jnp.float32(1.0), jnp.float32(0.0))
        dout_ref[f] = ((cot_ref[f].astype(jnp.float32) * used) * scale).astype(jnp.bfloat16)

    spread(dout_ref, taps, width)
    for kt in range(3):
        for tap in range(9):
            flipped[tap * channels : (tap + 1) * channels, kt * inner : (kt + 1) * inner] = weight_ref[kt, 8 - tap].T
    back[...] = jnp.zeros_like(back)

    @pl.loop(0, count // 2)
    def _(g):
        f = g * 2
        part = jnp.dot(
            taps[pl.ds(f, 2)].reshape(2 * pixels, 9 * channels), flipped[...], preferred_element_type=jnp.float32
        ).reshape(2, pixels, 3 * inner)
        for kt in range(3):
            back[pl.ds(f + kt, 2)] += part[:, :, kt * inner : (kt + 1) * inner]

    head_ref[...] = back[:2].astype(jnp.bfloat16)
    tail_ref[...] = back[2:]


def forward_kernel(
    width, scalars_ref, ext_ref, one_ref, two_ref, dout_ref, feat_ref, pre_ref, grad_ref, taps, turned, pre, hidden
):
    total, pixels, channels = ext_ref.shape
    count = total - 4
    inner = one_ref.shape[2]
    outer_channels = two_ref.shape[2]
    keep, valid = (scalars_ref[0], scalars_ref[1])
    spread(ext_ref, taps, width)
    pre[...] = jnp.zeros_like(pre)

    @pl.loop(0, total // 2)
    def _(g):
        f = g * 2
        weight = jnp.concatenate([one_ref[0], one_ref[1], one_ref[2]], axis=1)
        part = jnp.dot(
            taps[pl.ds(f, 2)].reshape(2 * pixels, 9 * channels), weight, preferred_element_type=jnp.float32
        ).reshape(2, pixels, 3 * inner)
        for kt in range(3):
            pre[pl.ds(f + 2 - kt, 2)] += part[:, :, kt * inner : (kt + 1) * inner]

    pre_ref[...] = pre[4 : 4 + count]

    @pl.loop(0, count + 2)
    def _(f):
        value = pre[f + 2]
        held = jnp.where((f >= 2) | (keep > 0), jnp.float32(1.0), jnp.float32(0.0))
        hidden[f] = (jax.nn.silu(value) * held).astype(jnp.bfloat16)

    spread(hidden, taps, width)

    @pl.loop(0, count // 2)
    def _(g):
        f = g * 2
        total_out = jnp.zeros((2 * pixels, outer_channels), jnp.float32)
        for kt in range(3):
            total_out += jnp.dot(
                taps[pl.ds(f + kt, 2)].reshape(2 * pixels, 9 * inner), two_ref[kt], preferred_element_type=jnp.float32
            )
        total_out = total_out.reshape(2, pixels, outer_channels)
        for i in range(2):
            used = jnp.broadcast_to(f + i < valid, (pixels, outer_channels))
            feat_ref[f + i] = jnp.where(used, total_out[i], 0.0).astype(jnp.bfloat16)

    turn(taps, 0, turned, inner)
    outer(turned, dout_ref, grad_ref, pixels)


def last_kernel(width, ext_ref, pre_ref, tail_ref, carried_ref, grad_ref, taps, turned, dpre):
    count, pixels, inner = pre_ref.shape
    channels = ext_ref.shape[2]
    spread(ext_ref.at[pl.ds(2, count + 2)], taps, width)
    turn(taps, 0, turned, channels)

    @pl.loop(0, count)
    def _(f):
        dhid = tail_ref[f]
        more = carried_ref[jnp.maximum(f - (count - 2), 0)].astype(jnp.float32)
        dhid = dhid + jnp.where(jnp.broadcast_to(f >= count - 2, more.shape), more, 0.0)
        at = pl.ds(pl.multiple_of(f * pixels, pixels), pixels)
        dpre[at, :] = (dhid * silu_slope(pre_ref[f])).astype(jnp.bfloat16)

    outer(turned, dpre, grad_ref, pixels)


def silu_slope(value):
    sig = jax.nn.sigmoid(value)
    return sig * (1.0 + value * (1.0 - sig))


VMEM = pl.BlockSpec(memory_space=pltpu.VMEM)
SMEM = pl.BlockSpec(memory_space=pltpu.SMEM)
PARAMS = pltpu.CompilerParams(vmem_limit_bytes=56 * 1024 * 1024)


def local(frames, clip_blocks, tail_frames, weight_one, weight_two, cotangent):
    count, height, width, channels = frames.shape
    pixels = height * width
    inner = weight_one.shape[-1]
    wide = weight_two.shape[-1]
    bf16, f32 = (jnp.bfloat16, jnp.float32)
    devices = lax.axis_size("dp")
    place = lax.axis_index("dp")
    frames = frames.reshape(count, pixels, channels)
    cotangent = cotangent.reshape(count, pixels, wide)
    one = weight_one.reshape(3, 9 * channels, inner)
    arrived = from_behind(frames[count - 4 :], "dp", 1)
    order = jnp.arange(clip_blocks.shape[0])
    ends = jnp.sum(jnp.where(order[None, :] <= order[:, None], clip_blocks[None, :], 0), axis=1)
    keep = jnp.where(jnp.any(ends - clip_blocks == place), 0, 1).astype(jnp.int32)
    last_match = ends - 1 == place
    tail_here = jnp.sum(jnp.where(last_match, tail_frames, 0))
    valid = jnp.where(jnp.any(last_match), tail_here, count).astype(jnp.int32)
    scalars = jnp.stack([keep, valid])
    scale = 1.0 / math.sqrt(devices * count * pixels)

    dout, head, tail = pl.pallas_call(
        functools.partial(back_kernel, width, scale),
        out_shape=(
            jax.ShapeDtypeStruct((count, pixels, wide), bf16),
            jax.ShapeDtypeStruct((2, pixels, inner), bf16),
            jax.ShapeDtypeStruct((count, pixels, inner), f32),
        ),
        in_specs=[SMEM, VMEM, VMEM],
        out_specs=(VMEM, VMEM, VMEM),
        scratch_shapes=[
            pltpu.VMEM((count, pixels, 9 * wide), bf16),
            pltpu.VMEM((9 * wide, 3 * inner), bf16),
            pltpu.VMEM((count + 2, pixels, inner), f32),
        ],
        compiler_params=PARAMS,
        cost_estimate=pl.CostEstimate(flops=10**10, bytes_accessed=5 * 10**6, transcendentals=0),
    )(scalars[1:], cotangent, weight_two.reshape(3, 9, inner, wide))
    carried = from_behind(head * keep.astype(bf16), "dp", -1)
    ext = jnp.concatenate([arrived * keep.astype(bf16), frames], axis=0)
    features, pre, grad_two = pl.pallas_call(
        functools.partial(forward_kernel, width),
        out_shape=(
            jax.ShapeDtypeStruct((count, pixels, wide), bf16),
            jax.ShapeDtypeStruct((count, pixels, inner), f32),
            jax.ShapeDtypeStruct((3, 9 * inner, wide), f32),
        ),
        in_specs=[SMEM, VMEM, VMEM, VMEM, VMEM],
        out_specs=(VMEM, VMEM, VMEM),
        scratch_shapes=[
            pltpu.VMEM((count + 4, pixels, 9 * max(channels, inner)), bf16),
            pltpu.VMEM((9 * inner, (count + 2) * pixels), bf16),
            pltpu.VMEM((count + 6, pixels, inner), f32),
            pltpu.VMEM((count + 2, pixels, inner), bf16),
        ],
        compiler_params=PARAMS,
        cost_estimate=pl.CostEstimate(flops=12 * 10**9, bytes_accessed=12 * 10**6, transcendentals=0),
    )(scalars, ext, one, weight_two.reshape(3, 9 * inner, wide), dout.reshape(count * pixels, wide))
    grad_one = pl.pallas_call(
        functools.partial(last_kernel, width),
        out_shape=jax.ShapeDtypeStruct((3, 9 * channels, inner), f32),
        in_specs=[VMEM] * 4,
        out_specs=VMEM,
        scratch_shapes=[
            pltpu.VMEM((count + 2, pixels, 9 * channels), bf16),
            pltpu.VMEM((9 * channels, (count + 2) * pixels), bf16),
            pltpu.VMEM((count * pixels, inner), bf16),
        ],
        compiler_params=PARAMS,
        cost_estimate=pl.CostEstimate(flops=4 * 10**9, bytes_accessed=5 * 10**6, transcendentals=0),
    )(ext, pre, tail, carried)
    grad_one, grad_two = sum_over_devices(grad_one, grad_two)
    return (
        features.reshape(count, height, width, wide),
        grad_one.reshape(weight_one.shape),
        grad_two.reshape(weight_two.shape),
    )


def solution(mesh):
    return jax.shard_map(
        local,
        mesh=mesh,
        in_specs=(P("dp", None, None, None), P(), P(), P(), P(), P("dp", None, None, None)),
        out_specs=(P("dp", None, None, None), P(), P()),
        check_vma=False,
    )
```

profile of v0, /device:TPU:0, one launch (start us, length us, event | category | flops | bytes accessed | tf_op | source)
XLA Modules:
  0.0 113.2 jit_solution(5360003709012832483)
XLA Ops:
  0.6 1.0 slice.18
  1.6 2.4 %collective-permute-start = (bf16[4,256,128]{2,1,0:T(8,128)(2,1)S(1)}, bf16[4,256,128]{2,1,0:T(8,128)(2,1)S(1)}, u32[]{:S(2)}, u32[]{:S(2)}) collective-permute-start(bf16[4,256,128]{2,1,0:T(8,128)(2,1)S(1)} %bitcast.21), channel_id=1, source_target_pairs={{0,1},{1,2},{2,3},{3,4},{4,5},{5,6},{6,7},{7,8},{8,9},{9,10},{10,1... | collective-permute-start | bytes 786440 | tf_op jit(solution)/shard_map/ppermute | solution.py:149
  4.0 0.8 select_reduce_fusion
  4.8 1.3 %compare_reduce_fusion = (pred[]{:T(512)}, pred[]{:T(512)}) fusion(s32[4]{0:T(128)S(1)} %select_reduce_fusion, s32[4]{0:T(128)} %param.7, s32[]{:T(128)S(6)} %axis_index.12), kind=kLoop, calls=%fused_computation.7 | loop fusion | flops 22 | bytes 38 | tf_op jit(solution)/shard_map/reduce_or | solution.py:315
  6.1 1.3 %fusion = s32[]{:T(128)} fusion(s32[4]{0:T(128)} %param.8, s32[4]{0:T(128)S(1)} %select_reduce_fusion, s32[]{:T(128)S(6)} %axis_index.12), kind=kLoop, calls=%fused_computation.10 | loop fusion | flops 15 | bytes 40 | tf_op jit(solution)/shard_map/reduce_sum | solution.py:317
  9.3 0.0 copy-start.2
  9.3 10.1 %shard_map.85 = (bf16[8,256,256]{2,1,0:T(8,128)(2,1)}, bf16[2,256,128]{2,1,0:T(8,128)(2,1)}, f32[8,256,128]{2,1,0:T(8,128)}) custom-call(s32[1]{0:T(128)} %bitcast.1.valid_ref, bf16[8,256,256]{2,1,0:T(8,128)(2,1)} %bitcast.24, bf16[3,9,128,256]{3,2,1,0:T(8,128)(2,1)} %bitcast.22), custom_call_target="tpu_custom_call" | custom-call | flops 10000000000 | bytes 5000000 | tf_op jit(solution)/shard_map/pallas_call | solution.py:322
  19.4 0.9 broadcast_multiply_fusion.1
  20.4 1.3 %collective-permute-start.1 = (bf16[2,256,128]{2,1,0:T(8,128)(2,1)S(1)}, bf16[2,256,128]{2,1,0:T(8,128)(2,1)S(1)}, u32[]{:S(2)}, u32[]{:S(2)}) collective-permute-start(bf16[2,256,128]{2,1,0:T(8,128)(2,1)S(1)} %broadcast_multiply_fusion.1), channel_id=1, source_target_pairs={{1,0},{2,1},{3,2},{4,3},{5,4},{6,5},{7,6},{8,7},{9,8},{10,9},{11,1... | collective-permute-start | bytes 393224 | tf_op jit(solution)/shard_map/ppermute | solution.py:149
  21.7 0.6 pad_add_fusion.scalars_ref
  22.3 0.0 collective-permute-done
  22.3 0.0 copy-done.2
  22.4 1.0 pad_maximum_fusion.1.ext_ref
  23.3 23.2 %shard_map.86 = (bf16[8,256,256]{2,1,0:T(8,128)(2,1)}, f32[8,256,128]{2,1,0:T(8,128)}, f32[3,1152,256]{2,1,0:T(8,128)}) custom-call(s32[2]{0:T(128)} %pad_add_fusion.scalars_ref, bf16[12,256,128]{2,1,0:T(8,128)(2,1)} %pad_maximum_fusion.1.ext_ref, bf16[3,1152,128]{2,1,0:T(8,128)(2,1)} %bitcast.25, bf16[3,1152,256]{2,1,0:T(8,128)(2,1)} %bitcast.23, ...), custom_call_target="tpu_custom_call" | custom-call | flops 12000000000 | bytes 12000000 | tf_op jit(solution)/shard_map/pallas_call | solution.py:341
  46.5 0.0 collective-permute-done.1.carried_ref
  46.5 0.0 copy-start.3
  46.5 0.6 copy-done.3
  47.2 0.0 copy-start
  47.2 11.6 %shard_map.87 = f32[3,1152,128]{2,1,0:T(8,128)} custom-call(bf16[12,256,128]{2,1,0:T(8,128)(2,1)} %pad_maximum_fusion.1.ext_ref, f32[8,256,128]{2,1,0:T(8,128)} %get-tuple-element.11.pre_ref, f32[8,256,128]{2,1,0:T(8,128)} %get-tuple-element.12.tail_ref, bf16[2,256,128]{2,1,0:T(8,128)(2,1)} %copy-done.3), custom_call_target="tpu_custom_call" | custom-call | flops 4000000000 | bytes 5000000 | tf_op jit(solution)/shard_map/pallas_call | solution.py:359
  58.7 0.0 copy-done
  58.7 0.0 copy-start.1
  58.8 1.5 %copy-done.1 = f32[3,1152,128]{2,1,0:T(8,128)S(1)} copy-done((f32[3,1152,128]{2,1,0:T(8,128)S(1)}, f32[3,1152,128]{2,1,0:T(8,128)}, u32[]{:S(2)}) %copy-start.1) | copy-done | bytes 1769496
  60.2 49.0 %shard_map.88 = bf16[3,3584,128]{2,1,0:T(8,128)(2,1)S(1)} custom-call(f32[3456,128]{1,0:T(8,128)S(1)} %bitcast.16, f32[3456,256]{1,0:T(8,128)S(1)} %bitcast.15), custom_call_target="tpu_custom_call" | custom-call | tf_op jit(solution)/shard_map/pallas_call | solution.py:123
  109.3 0.3 slice_convert_fusion
  109.6 1.5 %fusion.1 = (f32[1,3456,128]{2,1,0:T(8,128)S(1)}, f32[1,3456,128]{2,1,0:T(8,128)S(1)}, f32[1,3456,128]{2,1,0:T(8,128)}) fusion(f32[3,3456,128]{2,1,0:T(8,128)S(1)} %slice_convert_fusion), kind=kLoop, calls=%fused_computation.12 | loop fusion | bytes 10616832 | tf_op jit(solution)/shard_map/slice | solution.py:140
  111.2 2.1 %pad_maximum_fusion = f32[3,3,3,128,256]{4,3,2,1,0:T(8,128)} fusion(f32[3,3,3,128,128]{4,3,2,1,0:T(8,128)S(1)} %bitcast.18, f32[3,3,3,128,128]{4,3,2,1,0:T(8,128)S(1)} %bitcast.17), kind=kLoop, calls=%fused_computation | loop fusion | flops 884736 | bytes 7077888 | tf_op jit(solution)/shard_map/concatenate | solution.py:142
  (1 shorter events, 0.0 us)
Async XLA Ops:
  1.6 20.7 %collective-permute-start = (bf16[4,256,128]{2,1,0:T(8,128)(2,1)S(1)}, bf16[4,256,128]{2,1,0:T(8,128)(2,1)S(1)}, u32[]{:S(2)}, u32[]{:S(2)}) collective-permute-start(bf16[4,256,128]{2,1,0:T(8,128)(2,1)S(1)} %bitcast.21), channel_id=1, source_target_pairs={{0,1},{1,2},{2,3},{3,4},{4,5},{5,6},{6,7},{7,8},{8,9},{9,10},{10,1... | collective-permute-start | bytes 786440 | tf_op jit(solution)/shard_map/ppermute | solution.py:149
  9.3 13.0 %copy-start.2 = (bf16[8,16,16,128]{3,2,1,0:T(8,128)(2,1)S(1)}, bf16[8,16,16,128]{3,2,1,0:T(8,128)(2,1)}, u32[]{:S(2)}) copy-start(bf16[8,16,16,128]{3,2,1,0:T(8,128)(2,1)} %param.6) | copy-start | bytes 1572868
  20.4 26.1 %collective-permute-start.1 = (bf16[2,256,128]{2,1,0:T(8,128)(2,1)S(1)}, bf16[2,256,128]{2,1,0:T(8,128)(2,1)S(1)}, u32[]{:S(2)}, u32[]{:S(2)}) collective-permute-start(bf16[2,256,128]{2,1,0:T(8,128)(2,1)S(1)} %broadcast_multiply_fusion.1), channel_id=1, source_target_pairs={{1,0},{2,1},{3,2},{4,3},{5,4},{6,5},{7,6},{8,7},{9,8},{10,9},{11,1... | collective-permute-start | bytes 393224 | tf_op jit(solution)/shard_map/ppermute | solution.py:149
  46.5 0.6 copy-start.3
  47.2 11.6 %copy-start = (f32[3,1152,256]{2,1,0:T(8,128)S(1)}, f32[3,1152,256]{2,1,0:T(8,128)}, u32[]{:S(2)}) copy-start(f32[3,1152,256]{2,1,0:T(8,128)} %get-tuple-element.14) | copy-start | bytes 10616836
  58.7 1.5 %copy-start.1 = (f32[3,1152,128]{2,1,0:T(8,128)S(1)}, f32[3,1152,128]{2,1,0:T(8,128)}, u32[]{:S(2)}) copy-start(f32[3,1152,128]{2,1,0:T(8,128)} %shard_map.87) | copy-start | bytes 5308420
where the time goes:
time: 114 us; the launch traced here: 113 us
  Pallas kernels  93.9 us (82%)
  other arithmetic  8.35 us (7%)
  local copies, waits for them, and re-layouts  4.65 us (4%)
  starting transfers between devices  3.66 us (3%)
  between operations  2.66 us (2%)
    pallas_call x1, Pallas kernels, sum_over_devices(): pl.pallas_call(functools.partial(sum_kernel, levels), out_shape=jax.Shape...  49 us
    pallas_call x1, Pallas kernels, local(): pl.pallas_call(functools.partial(forward_kernel, width), out_shape=(jax.S...  23.2 us
    pallas_call x1, Pallas kernels, local(): pl.pallas_call(functools.partial(last_kernel, width), out_shape=jax.Shape...  11.6 us
    pallas_call x1, Pallas kernels, local(): pl.pallas_call(functools.partial(back_kernel, width, scale), out_shape=(j...  10.1 us
    ppermute x2, starting transfers between devices, from_behind(): lax.ppermute(value, axis, [(source, source + steps) for source in range(i...  3.66 us
  transfers between devices with their start and end apart: 2, of which 0 were waited for; matrix products, arithmetic and copies ran while one was open for 5% of the time, Pallas kernels for 29%

commit v1 on v0

--- a/solution.py
+++ b/solution.py
@@ -17,9 +17,31 @@
     return [0] + middle[turn:] + middle[:turn] + [levels - 1]
 
 
-def sum_kernel(levels, one_ref, two_ref, out_ref, acc, sent, came, rs_send, rs_recv, ag_send, ag_recv):
+def sum_kernel(
+    levels,
+    width,
+    ext_ref,
+    pre_ref,
+    tail_ref,
+    carried_ref,
+    two_ref,
+    out_one,
+    out_two,
+    acc,
+    sent,
+    came,
+    taps,
+    turned,
+    dpre,
+    rs_send,
+    rs_recv,
+    ag_send,
+    ag_recv,
+):
     chunks, rows = (acc.shape[0], acc.shape[1])
-    real = one_ref.shape[0]
+    count, pixels, inner = pre_ref.shape
+    channels = ext_ref.shape[2]
+    real = two_ref.shape[0]
     me = lax.axis_index("dp")
     bits = [lax.rem(me // (1 << k), 2) for k in range(levels)]
     partners = [me + (1 - 2 * bits[k]) * (1 << k) for k in range(levels)]
@@ -29,10 +51,9 @@
     for k in range(levels):
         pl.semaphore_signal(barrier, inc=1, device_id=(partners[k],), device_id_type=pl.DeviceIdType.MESH)
 
-    wide = one_ref.shape[1] // LANES
     for chunk in range(chunks):
-        ref, col = (one_ref, chunk) if chunk < wide else (two_ref, chunk - wide)
-        acc[chunk, :real, :] = ref[:, col * LANES : (col + 1) * LANES]
+        if chunk:
+            acc[chunk, :real, :] = two_ref[:, (chunk - 1) * LANES : chunk * LANES]
         if rows > real:
             acc[chunk, real:, :] = jnp.zeros((rows - real, LANES), jnp.float32)
 
@@ -40,6 +61,12 @@
 
     def aligned(value):
         return pl.multiple_of(value, 16)
+
+    def landing(chunk, base, size):
+        at = pl.ds(aligned(base), size)
+        if chunk == 0:
+            return out_one.at[at, :]
+        return out_two.at[at, (chunk - 1) * LANES : chunk * LANES]
 
     def scatter_copy(chunk, step):
         size = rows >> (step + 1)
@@ -56,8 +83,8 @@
     def gather_copy(chunk, step, base):
         size = rows >> (step + 1)
         return pltpu.make_async_remote_copy(
-            src_ref=out_ref.at[chunk, pl.ds(aligned(base), size)],
-            dst_ref=out_ref.at[chunk, pl.ds(aligned(base), size)],
+            src_ref=landing(chunk, base, size),
+            dst_ref=landing(chunk, base, size),
             send_sem=ag_send.at[chunk, step],
             recv_sem=ag_recv.at[chunk, step],
             device_id=(partners[orders[chunk][step]],),
@@ -67,6 +94,11 @@
     base = [jnp.int32(0)] * chunks
     copies = [None] * chunks
     pending = []
+
+    def start(chunk, copy):
+        copies[chunk] = copy
+        copy.start()
+        pending.append(copy)
 
     def send_half(chunk, step):
         size = rows >> (step + 1)
@@ -74,73 +106,107 @@
         bit = bits[orders[chunk][step]]
         away = aligned(base[chunk] + (1 - bit) * size)
         sent[chunk, pl.ds(at, size), :] = acc[chunk, pl.ds(away, size), :].astype(jnp.bfloat16)
-        copies[chunk] = scatter_copy(chunk, step)
-        copies[chunk].start()
-        pending.append(copies[chunk])
+        start(chunk, scatter_copy(chunk, step))
         base[chunk] = base[chunk] + bit * size
 
-    for chunk in range(chunks):
-        send_half(chunk, 0)
-    for step in range(levels):
+    def scatter_step(chunk, step):
         size = rows >> (step + 1)
         at = rows - (rows >> step)
+        copies[chunk].wait_recv()
+        here = pl.ds(aligned(base[chunk]), size)
+        total = acc[chunk, here, :] + came[chunk, pl.ds(at, size), :].astype(jnp.float32)
+        if step + 1 < levels:
+            acc[chunk, here, :] = total
+            send_half(chunk, step + 1)
+        else:
+            landing(chunk, base[chunk], size)[...] = total.astype(jnp.bfloat16)
+            start(chunk, gather_copy(chunk, step, base[chunk]))
+
+    def gather_step(chunk, step):
+        size = rows >> (step + 1)
+        copies[chunk].wait_recv()
+        base[chunk] = base[chunk] - bits[orders[chunk][step]] * size
+        if step > 0:
+            start(chunk, gather_copy(chunk, step - 1, base[chunk]))
+
+    def steps(chunk):
+        work = [functools.partial(send_half, chunk, 0)]
+        work += [functools.partial(scatter_step, chunk, step) for step in range(levels)]
+        return work + [functools.partial(gather_step, chunk, step) for step in reversed(range(levels))]
+
+    def slope_part():
+        @pl.loop(0, count)
+        def _(f):
+            dhid = tail_ref[f]
+            more = carried_ref[jnp.maximum(f - (count - 2), 0)].astype(jnp.float32)
+            dhid = dhid + jnp.where(jnp.broadcast_to(f >= count - 2, more.shape), more, 0.0)
+            at = pl.ds(pl.multiple_of(f * pixels, pixels), pixels)
+            dpre[at, :] = (dhid * silu_slope(pre_ref[f])).astype(jnp.bfloat16)
+
+    def outer_part(kt):
+        height = turned.shape[0] // 3
+
+        @pl.loop(0, 3)
+        def _(kh):
+            at = pl.ds(pl.multiple_of(kh * height, height), height)
+            into = pl.ds(pl.multiple_of((kt * 3 + kh) * height, height), height)
+            acc[0, into, :] = jnp.dot(
+                turned[at, kt * pixels : kt * pixels + count * pixels], dpre[...], preferred_element_type=jnp.float32
+            )
+
+    local = [
+        functools.partial(spread, ext_ref.at[pl.ds(2, count + 2)], taps, width),
+        functools.partial(turn, taps, 0, turned, channels),
+        slope_part,
+    ] + [functools.partial(outer_part, kt) for kt in range(3)]
+    queues = [steps(chunk) for chunk in range(chunks)]
+    for part in local:
+        for chunk in range(1, chunks):
+            if queues[chunk]:
+                queues[chunk].pop(0)()
+        part()
+    while any(queues):
         for chunk in range(chunks):
-            copies[chunk].wait_recv()
-            here = pl.ds(aligned(base[chunk]), size)
-            total = acc[chunk, here, :] + came[chunk, pl.ds(at, size), :].astype(jnp.float32)
-            if step + 1 < levels:
-                acc[chunk, here, :] = total
-                send_half(chunk, step + 1)
-            else:
-                out_ref[chunk, here, :] = total.astype(jnp.bfloat16)
-                copies[chunk] = gather_copy(chunk, step, base[chunk])
-                copies[chunk].start()
-                pending.append(copies[chunk])
-    for step in reversed(range(levels)):
-        size = rows >> (step + 1)
-        for chunk in range(chunks):
-            copies[chunk].wait_recv()
-            base[chunk] = base[chunk] - bits[orders[chunk][step]] * size
-            if step > 0:
-                copies[chunk] = gather_copy(chunk, step - 1, base[chunk])
-                copies[chunk].start()
-                pending.append(copies[chunk])
+            if queues[chunk]:
+                queues[chunk].pop(0)()
     for copy in pending:
         copy.wait_send()
 
 
-def sum_over_devices(one, two):
+def sum_over_devices(width, ext, pre, tail, carried, two):
     devices = lax.axis_size("dp")
     levels = devices.bit_length() - 1
     assert devices == 1 << levels
-    shape_one, shape_two = (one.shape, two.shape)
-    one = one.reshape(-1, one.shape[-1])
+    count, pixels, inner = pre.shape
+    channels = ext.shape[2]
+    assert inner == LANES
     two = two.reshape(-1, two.shape[-1])
-    real = one.shape[0]
+    real, wide = two.shape
     step = 16 * devices
     rows = -(-real // step) * step
-    chunks = (one.shape[1] + two.shape[1]) // LANES
-    summed = pl.pallas_call(
-        functools.partial(sum_kernel, levels),
-        out_shape=jax.ShapeDtypeStruct((chunks, rows, LANES), jnp.bfloat16),
-        in_specs=[pl.BlockSpec(memory_space=pltpu.VMEM)] * 2,
-        out_specs=pl.BlockSpec(memory_space=pltpu.VMEM),
+    chunks = 1 + wide // LANES
+    one, two = pl.pallas_call(
+        functools.partial(sum_kernel, levels, width),
+        out_shape=(
+            jax.ShapeDtypeStruct((rows, LANES), jnp.bfloat16),
+            jax.ShapeDtypeStruct((rows, wide), jnp.bfloat16),
+        ),
+        in_specs=[pl.BlockSpec(memory_space=pltpu.VMEM)] * 5,
+        out_specs=(pl.BlockSpec(memory_space=pltpu.VMEM),) * 2,
         scratch_shapes=[
             pltpu.VMEM((chunks, rows, LANES), jnp.float32),
             pltpu.VMEM((chunks, rows, LANES), jnp.bfloat16),
             pltpu.VMEM((chunks, rows, LANES), jnp.bfloat16),
+            pltpu.VMEM((count + 2, pixels, 9 * channels), jnp.bfloat16),
+            pltpu.VMEM((9 * channels, (count + 2) * pixels), jnp.bfloat16),
+            pltpu.VMEM((count * pixels, inner), jnp.bfloat16),
         ]
         + [pltpu.SemaphoreType.DMA((chunks, levels))] * 4,
         compiler_params=pltpu.CompilerParams(
-            collective_id=0, has_side_effects=True, vmem_limit_bytes=40 * 1024 * 1024
+            collective_id=0, has_side_effects=True, vmem_limit_bytes=56 * 1024 * 1024
         ),
-    )(one, two)
-    summed = summed[:, :real].astype(jnp.float32)
-    wide = one.shape[1] // LANES
-    whole = [summed[chunk] for chunk in range(chunks)]
-    grad_one = jnp.concatenate(whole[:wide], axis=1).reshape(shape_one)
-    grad_two = jnp.concatenate(whole[wide:], axis=1).reshape(shape_two)
-    return grad_one, grad_two
+    )(ext, pre, tail, carried, two)
+    return one[:real].astype(jnp.float32), two[:real].astype(jnp.float32)
 
 
 def from_behind(value, axis, steps):
@@ -194,10 +260,20 @@
             )
 
 
-def back_kernel(width, scale, valid_ref, cot_ref, weight_ref, dout_ref, head_ref, tail_ref, taps, flipped, back):
+def clip_place(blocks_ref, tails_ref, count):
+    place = lax.axis_index("dp")
+    start, keep, valid = (jnp.int32(0), jnp.int32(1), jnp.int32(count))
+    for clip in range(blocks_ref.shape[0]):
+        keep = jnp.where(start == place, 0, keep)
+        start = start + blocks_ref[clip]
+        valid = jnp.where(start - 1 == place, tails_ref[clip], valid)
+    return keep, valid
+
+
+def back_kernel(width, scale, blocks_ref, tails_ref, cot_ref, weight_ref, dout_ref, head_ref, tail_ref, taps, flipped, back):
     count, pixels, channels = cot_ref.shape
     inner = tail_ref.shape[2]
-    valid = valid_ref[0]
+    keep, valid = clip_place(blocks_ref, tails_ref, count)
 
     @pl.loop(0, count)
     def _(f):
@@ -219,18 +295,37 @@
         for kt in range(3):
             back[pl.ds(f + kt, 2)] += part[:, :, kt * inner : (kt + 1) * inner]
 
-    head_ref[...] = back[:2].astype(jnp.bfloat16)
+    held = jnp.where(keep > 0, jnp.float32(1.0), jnp.float32(0.0))
+    head_ref[...] = (back[:2] * held).astype(jnp.bfloat16)
     tail_ref[...] = back[2:]
 
 
 def forward_kernel(
-    width, scalars_ref, ext_ref, one_ref, two_ref, dout_ref, feat_ref, pre_ref, grad_ref, taps, turned, pre, hidden
+    width,
+    blocks_ref,
+    tails_ref,
+    arrived_ref,
+    frames_ref,
+    one_ref,
+    two_ref,
+    dout_ref,
+    feat_ref,
+    pre_ref,
+    grad_ref,
+    ext_ref,
+    taps,
+    turned,
+    pre,
+    hidden,
 ):
     total, pixels, channels = ext_ref.shape
     count = total - 4
     inner = one_ref.shape[2]
     outer_channels = two_ref.shape[2]
-    keep, valid = (scalars_ref[0], scalars_ref[1])
+    keep, valid = clip_place(blocks_ref, tails_ref, count)
+    arrived = arrived_ref[...].astype(jnp.float32) * jnp.where(keep > 0, jnp.float32(1.0), jnp.float32(0.0))
+    ext_ref[:4] = arrived.astype(jnp.bfloat16)
+    ext_ref[4:] = frames_ref[...]
     spread(ext_ref, taps, width)
     pre[...] = jnp.zeros_like(pre)
 
@@ -271,23 +366,6 @@
     outer(turned, dout_ref, grad_ref, pixels)
 
 
-def last_kernel(width, ext_ref, pre_ref, tail_ref, carried_ref, grad_ref, taps, turned, dpre):
-    count, pixels, inner = pre_ref.shape
-    channels = ext_ref.shape[2]
-    spread(ext_ref.at[pl.ds(2, count + 2)], taps, width)
-    turn(taps, 0, turned, channels)
-
-    @pl.loop(0, count)
-    def _(f):
-        dhid = tail_ref[f]
-        more = carried_ref[jnp.maximum(f - (count - 2), 0)].astype(jnp.float32)
-        dhid = dhid + jnp.where(jnp.broadcast_to(f >= count - 2, more.shape), more, 0.0)
-        at = pl.ds(pl.multiple_of(f * pixels, pixels), pixels)
-        dpre[at, :] = (dhid * silu_slope(pre_ref[f])).astype(jnp.bfloat16)
-
-    outer(turned, dpre, grad_ref, pixels)
-
-
 def silu_slope(value):
     sig = jax.nn.sigmoid(value)
     return sig * (1.0 + value * (1.0 - sig))
@@ -305,18 +383,10 @@
     wide = weight_two.shape[-1]
     bf16, f32 = (jnp.bfloat16, jnp.float32)
     devices = lax.axis_size("dp")
-    place = lax.axis_index("dp")
     frames = frames.reshape(count, pixels, channels)
     cotangent = cotangent.reshape(count, pixels, wide)
     one = weight_one.reshape(3, 9 * channels, inner)
     arrived = from_behind(frames[count - 4 :], "dp", 1)
-    order = jnp.arange(clip_blocks.shape[0])
-    ends = jnp.sum(jnp.where(order[None, :] <= order[:, None], clip_blocks[None, :], 0), axis=1)
-    keep = jnp.where(jnp.any(ends - clip_blocks == place), 0, 1).astype(jnp.int32)
-    last_match = ends - 1 == place
-    tail_here = jnp.sum(jnp.where(last_match, tail_frames, 0))
-    valid = jnp.where(jnp.any(last_match), tail_here, count).astype(jnp.int32)
-    scalars = jnp.stack([keep, valid])
     scale = 1.0 / math.sqrt(devices * count * pixels)
 
     dout, head, tail = pl.pallas_call(
@@ -326,7 +396,7 @@
             jax.ShapeDtypeStruct((2, pixels, inner), bf16),
             jax.ShapeDtypeStruct((count, pixels, inner), f32),
         ),
-        in_specs=[SMEM, VMEM, VMEM],
+        in_specs=[SMEM, SMEM, VMEM, VMEM],
         out_specs=(VMEM, VMEM, VMEM),
         scratch_shapes=[
             pltpu.VMEM((count, pixels, 9 * wide), bf16),
@@ -335,18 +405,18 @@
         ],
         compiler_params=PARAMS,
         cost_estimate=pl.CostEstimate(flops=10**10, bytes_accessed=5 * 10**6, transcendentals=0),
-    )(scalars[1:], cotangent, weight_two.reshape(3, 9, inner, wide))
-    carried = from_behind(head * keep.astype(bf16), "dp", -1)
-    ext = jnp.concatenate([arrived * keep.astype(bf16), frames], axis=0)
-    features, pre, grad_two = pl.pallas_call(
+    )(clip_blocks, tail_frames, cotangent, weight_two.reshape(3, 9, inner, wide))
+    carried = from_behind(head, "dp", -1)
+    features, pre, grad_two, ext = pl.pallas_call(
         functools.partial(forward_kernel, width),
         out_shape=(
             jax.ShapeDtypeStruct((count, pixels, wide), bf16),
             jax.ShapeDtypeStruct((count, pixels, inner), f32),
             jax.ShapeDtypeStruct((3, 9 * inner, wide), f32),
+            jax.ShapeDtypeStruct((count + 4, pixels, channels), bf16),
         ),
-        in_specs=[SMEM, VMEM, VMEM, VMEM, VMEM],
-        out_specs=(VMEM, VMEM, VMEM),
+        in_specs=[SMEM, SMEM, VMEM, VMEM, VMEM, VMEM, VMEM],
+        out_specs=(VMEM, VMEM, VMEM, VMEM),
         scratch_shapes=[
             pltpu.VMEM((count + 4, pixels, 9 * max(channels, inner)), bf16),
             pltpu.VMEM((9 * inner, (count + 2) * pixels), bf16),
@@ -355,21 +425,8 @@
         ],
         compiler_params=PARAMS,
         cost_estimate=pl.CostEstimate(flops=12 * 10**9, bytes_accessed=12 * 10**6, transcendentals=0),
-    )(scalars, ext, one, weight_two.reshape(3, 9 * inner, wide), dout.reshape(count * pixels, wide))
-    grad_one = pl.pallas_call(
-        functools.partial(last_kernel, width),
-        out_shape=jax.ShapeDtypeStruct((3, 9 * channels, inner), f32),
-        in_specs=[VMEM] * 4,
-        out_specs=VMEM,
-        scratch_shapes=[
-            pltpu.VMEM((count + 2, pixels, 9 * channels), bf16),
-            pltpu.VMEM((9 * channels, (count + 2) * pixels), bf16),
-            pltpu.VMEM((count * pixels, inner), bf16),
-        ],
-        compiler_params=PARAMS,
-        cost_estimate=pl.CostEstimate(flops=4 * 10**9, bytes_accessed=5 * 10**6, transcendentals=0),
-    )(ext, pre, tail, carried)
-    grad_one, grad_two = sum_over_devices(grad_one, grad_two)
+    )(clip_blocks, tail_frames, arrived, frames, one, weight_two.reshape(3, 9 * inner, wide), dout.reshape(count * pixels, wide))
+    grad_one, grad_two = sum_over_devices(width, ext, pre, tail, carried, grad_two)
     return (
         features.reshape(count, height, width, wide),
         grad_one.reshape(weight_one.shape),

time: 114 us -> 120 us (1.053)
  Pallas kernels: 93.9 us -> 108 us
  other arithmetic: 8.35 us -> 3.63 us
  between operations: 2.66 us -> 0.7 us
    pallas_call x2 -> x1, Pallas kernels: 60.6 us -> 74.2 us  [sum_over_devices(): pl.pallas_call(functools.partial(sum_kernel, levels, width), out_shape=(j...]
    reshape x0 -> x2, other arithmetic: none -> 3.63 us  [the longest x1 2.22 us: local(): grad_two.reshape(weight_two.shape)]
    concatenate x2 -> x0, other arithmetic: 3.06 us -> none  [the longest x1 2.08 us: sum_over_devices(): grad_two = jnp.concatenate(whole[wide:], axis=1).reshape(shape_two)]
    reduce_sum x2 -> x0, other arithmetic: 2.07 us -> none  [the longest x1 1.29 us: local(): tail_here = jnp.sum(jnp.where(last_match, tail_frames, 0))]
    reduce_or x1 -> x0, other arithmetic: 1.3 us -> none  [local(): jnp.any(ends - clip_blocks == place)]
  transfers between devices with their start and end apart: 2 -> 2, of which waited for: 0 -> 0; matrix products, arithmetic and copies ran while one was open for 5% -> 0% of each run, Pallas kernels for 29% -> 28%
where the time goes in v1:
time: 120 us
  Pallas kernels  108 us (90%)
  local copies, waits for them, and re-layouts  3.78 us (3%)
  starting transfers between devices  3.65 us (3%)
  other arithmetic  3.63 us (3%)
    pallas_call x1, Pallas kernels, sum_over_devices(): pl.pallas_call(functools.partial(sum_kernel, levels, width), out_shape=(j...  74.2 us
    pallas_call x1, Pallas kernels, local(): pl.pallas_call(functools.partial(forward_kernel, width), out_shape=(jax.S...  23.5 us
    pallas_call x1, Pallas kernels, local(): pl.pallas_call(functools.partial(back_kernel, width, scale), out_shape=(j...  10.1 us
    ppermute x2, starting transfers between devices, from_behind(): lax.ppermute(value, axis, [(source, source + steps) for source in range(i...  3.65 us
  transfers between devices with their start and end apart: 2, of which 0 were waited for; matrix products, arithmetic and copies ran while one was open for 0% of the time, Pallas kernels for 28%

profile of v1, /device:TPU:0, one launch (start us, length us, event | category | flops | bytes accessed | tf_op | source)
XLA Modules:
  0.0 119.5 jit_solution(4383138369428672986)
XLA Ops:
  0.6 1.0 slice.12
  1.6 2.4 %collective-permute-start = (bf16[4,256,128]{2,1,0:T(8,128)(2,1)S(1)}, bf16[4,256,128]{2,1,0:T(8,128)(2,1)S(1)}, u32[]{:S(2)}, u32[]{:S(2)}) collective-permute-start(bf16[4,256,128]{2,1,0:T(8,128)(2,1)S(1)} %bitcast.16), channel_id=1, source_target_pairs={{0,1},{1,2},{2,3},{3,4},{4,5},{5,6},{6,7},{7,8},{8,9},{9,10},{10,1... | collective-permute-start | bytes 786440 | tf_op jit(solution)/shard_map/ppermute | solution.py:215
  4.0 10.1 %shard_map.85 = (bf16[8,256,256]{2,1,0:T(8,128)(2,1)}, bf16[2,256,128]{2,1,0:T(8,128)(2,1)}, f32[8,256,128]{2,1,0:T(8,128)}) custom-call(s32[4]{0:T(128)} %blocks_ref.3, s32[4]{0:T(128)} %tails_ref.3, bf16[8,256,256]{2,1,0:T(8,128)(2,1)} %bitcast.20, bf16[3,9,128,256]{3,2,1,0:T(8,128)(2,1)} %bitcast.18), custom_call_target="tpu_custom_call" | custom-call | flops 10000000000 | bytes 5000000 | tf_op jit(solution)/shard_map/pallas_call | solution.py:392
  14.1 1.3 %collective-permute-start.1 = (bf16[2,256,128]{2,1,0:T(8,128)(2,1)}, bf16[2,256,128]{2,1,0:T(8,128)(2,1)S(1)}, u32[]{:S(2)}, u32[]{:S(2)}) collective-permute-start(bf16[2,256,128]{2,1,0:T(8,128)(2,1)} %get-tuple-element.17), channel_id=1, source_target_pairs={{1,0},{2,1},{3,2},{4,3},{5,4},{6,5},{7,6},{8,7},{9,8},{10,9},{11,1... | collective-permute-start | bytes 393224 | tf_op jit(solution)/shard_map/ppermute | solution.py:215
  15.4 0.0 collective-permute-done.arrived_ref
  15.4 0.0 copy-start.2
  15.4 0.7 copy-done.2
  16.1 23.5 %shard_map.86 = (bf16[8,256,256]{2,1,0:T(8,128)(2,1)}, f32[8,256,128]{2,1,0:T(8,128)}, f32[3,1152,256]{2,1,0:T(8,128)}, bf16[12,256,128]{2,1,0:T(8,128)(2,1)}) custom-call(s32[4]{0:T(128)} %blocks_ref.3, s32[4]{0:T(128)} %tails_ref.3, bf16[4,256,128]{2,1,0:T(8,128)(2,1)} %copy-done.2, bf16[8,256,128]{2,1,0:T(8,128)(2,1)} %bitcast.17, ...), custom_call_target="tpu_custom_call" | custom-call | flops 12000000000 | bytes 12000000 | tf_op jit(solution)/shard_map/pallas_call | solution.py:410
  39.5 0.0 collective-permute-done.1.carried_ref
  39.5 0.0 copy-start.1
  39.6 0.6 copy-done.1
  40.2 74.2 %shard_map.87 = (bf16[3584,128]{1,0:T(8,128)(2,1)}, bf16[3584,256]{1,0:T(8,128)(2,1)}) custom-call(bf16[12,256,128]{2,1,0:T(8,128)(2,1)} %get-tuple-element.14.ext_ref, f32[8,256,128]{2,1,0:T(8,128)} %get-tuple-element.15.pre_ref, f32[8,256,128]{2,1,0:T(8,128)} %get-tuple-element.16.tail_ref, bf16[2,256,128]{2,1,0:T(8,128)(2,1)} %copy-done.1, ...), custom_call_target="tpu_custom_call" | custom-call | tf_op jit(solution)/shard_map/pallas_call | solution.py:188
  114.4 0.0 copy-start
  114.4 1.4 %slice.14 = bf16[3456,128]{1,0:T(8,128)(2,1)S(1)} slice(bf16[3584,128]{1,0:T(8,128)(2,1)} %get-tuple-element.19), slice={[0:3456], [0:128]} | slice | bytes 1769472 | tf_op jit(solution)/shard_map/slice | solution.py:209
  115.8 1.4 %convert.2 = f32[3,3,3,128,128]{4,3,2,1,0:T(8,128)} convert(bf16[3,3,3,128,128]{4,3,2,1,0:T(8,128)(2,1)S(1)} %bitcast.15) | non-fusion elementwise | flops 442368 | bytes 2654208 | tf_op jit(solution)/shard_map/reshape | solution.py:432
  117.2 0.0 copy-done
  117.2 0.1 slice.15
  117.3 2.2 %convert.3 = f32[3,3,3,128,256]{4,3,2,1,0:T(8,128)} convert(bf16[3,3,3,128,256]{4,3,2,1,0:T(8,128)(2,1)S(1)} %bitcast.13) | non-fusion elementwise | flops 884736 | bytes 5308416 | tf_op jit(solution)/shard_map/reshape | solution.py:433
Async XLA Ops:
  1.6 13.8 %collective-permute-start = (bf16[4,256,128]{2,1,0:T(8,128)(2,1)S(1)}, bf16[4,256,128]{2,1,0:T(8,128)(2,1)S(1)}, u32[]{:S(2)}, u32[]{:S(2)}) collective-permute-start(bf16[4,256,128]{2,1,0:T(8,128)(2,1)S(1)} %bitcast.16), channel_id=1, source_target_pairs={{0,1},{1,2},{2,3},{3,4},{4,5},{5,6},{6,7},{7,8},{8,9},{9,10},{10,1... | collective-permute-start | bytes 786440 | tf_op jit(solution)/shard_map/ppermute | solution.py:215
  14.1 25.5 %collective-permute-start.1 = (bf16[2,256,128]{2,1,0:T(8,128)(2,1)}, bf16[2,256,128]{2,1,0:T(8,128)(2,1)S(1)}, u32[]{:S(2)}, u32[]{:S(2)}) collective-permute-start(bf16[2,256,128]{2,1,0:T(8,128)(2,1)} %get-tuple-element.17), channel_id=1, source_target_pairs={{1,0},{2,1},{3,2},{4,3},{5,4},{6,5},{7,6},{8,7},{9,8},{10,9},{11,1... | collective-permute-start | bytes 393224 | tf_op jit(solution)/shard_map/ppermute | solution.py:215
  15.4 0.7 copy-start.2
  39.5 0.7 copy-start.1
  114.4 2.8 %copy-start = (bf16[3584,256]{1,0:T(8,128)(2,1)S(1)}, bf16[3584,256]{1,0:T(8,128)(2,1)}, u32[]{:S(2)}) copy-start(bf16[3584,256]{1,0:T(8,128)(2,1)} %get-tuple-element.20) | copy-start | bytes 5505028

commit v2 on v1

--- a/solution.py
+++ b/solution.py
@@ -25,8 +25,7 @@
     tail_ref,
     carried_ref,
     two_ref,
-    out_one,
-    out_two,
+    out_ref,
     acc,
     sent,
     came,
@@ -64,9 +63,7 @@
 
     def landing(chunk, base, size):
         at = pl.ds(aligned(base), size)
-        if chunk == 0:
-            return out_one.at[at, :]
-        return out_two.at[at, (chunk - 1) * LANES : chunk * LANES]
+        return out_ref.at[chunk, at]
 
     def scatter_copy(chunk, step):
         size = rows >> (step + 1)
@@ -161,9 +158,6 @@
     ] + [functools.partial(outer_part, kt) for kt in range(3)]
     queues = [steps(chunk) for chunk in range(chunks)]
     for part in local:
-        for chunk in range(1, chunks):
-            if queues[chunk]:
-                queues[chunk].pop(0)()
         part()
     while any(queues):
         for chunk in range(chunks):
@@ -185,14 +179,11 @@
     step = 16 * devices
     rows = -(-real // step) * step
     chunks = 1 + wide // LANES
-    one, two = pl.pallas_call(
+    summed = pl.pallas_call(
         functools.partial(sum_kernel, levels, width),
-        out_shape=(
-            jax.ShapeDtypeStruct((rows, LANES), jnp.bfloat16),
-            jax.ShapeDtypeStruct((rows, wide), jnp.bfloat16),
-        ),
+        out_shape=jax.ShapeDtypeStruct((chunks, rows, LANES), jnp.bfloat16),
         in_specs=[pl.BlockSpec(memory_space=pltpu.VMEM)] * 5,
-        out_specs=(pl.BlockSpec(memory_space=pltpu.VMEM),) * 2,
+        out_specs=pl.BlockSpec(memory_space=pltpu.VMEM),
         scratch_shapes=[
             pltpu.VMEM((chunks, rows, LANES), jnp.float32),
             pltpu.VMEM((chunks, rows, LANES), jnp.bfloat16),
@@ -206,7 +197,8 @@
             collective_id=0, has_side_effects=True, vmem_limit_bytes=56 * 1024 * 1024
         ),
     )(ext, pre, tail, carried, two)
-    return one[:real].astype(jnp.float32), two[:real].astype(jnp.float32)
+    summed = summed[:, :real].astype(jnp.float32)
+    return summed[0], jnp.concatenate([summed[chunk] for chunk in range(1, chunks)], axis=1)
 
 
 def from_behind(value, axis, steps):

time: 120 us -> 108 us (0.900)
  Pallas kernels: 108 us -> 95.6 us
    pallas_call x1, Pallas kernels: 74.2 us -> 62 us  [sum_over_devices(): pl.pallas_call(functools.partial(sum_kernel, levels, width), out_shape=ja...]
    reshape x2 -> x0, other arithmetic: 3.63 us -> none  [the longest x1 2.22 us: local(): grad_two.reshape(weight_two.shape)]
    convert_element_type x0 -> x1, other arithmetic: none -> 2.1 us  [sum_over_devices(): summed = summed[:, :real].astype(jnp.float32)]
    concatenate x0 -> x1, other arithmetic: none -> 2.08 us  [sum_over_devices(): jnp.concatenate([summed[chunk] for chunk in range(1, chunks)], axis=1)]
  transfers between devices with their start and end apart: 2 -> 2, of which waited for: 0 -> 0; matrix products, arithmetic and copies ran while one was open for 0% -> 0% of each run, Pallas kernels for 28% -> 31%
where the time goes in v2:
time: 108 us
  Pallas kernels  95.6 us (89%)
  other arithmetic  4.17 us (4%)
  local copies, waits for them, and re-layouts  3.87 us (4%)
  starting transfers between devices  3.65 us (3%)
    pallas_call x1, Pallas kernels, sum_over_devices(): pl.pallas_call(functools.partial(sum_kernel, levels, width), out_shape=ja...  62 us
    pallas_call x1, Pallas kernels, local(): pl.pallas_call(functools.partial(forward_kernel, width), out_shape=(jax.S...  23.5 us
    pallas_call x1, Pallas kernels, local(): pl.pallas_call(functools.partial(back_kernel, width, scale), out_shape=(j...  10.1 us
    ppermute x2, starting transfers between devices, from_behind(): lax.ppermute(value, axis, [(source, source + steps) for source in range(i...  3.65 us
  transfers between devices with their start and end apart: 2, of which 0 were waited for; matrix products, arithmetic and copies ran while one was open for 0% of the time, Pallas kernels for 31%

profile of v2, /device:TPU:0, one launch (start us, length us, event | category | flops | bytes accessed | tf_op | source)
XLA Modules:
  0.0 107.9 jit_solution(254096673620292512)
XLA Ops:
  0.6 1.0 slice.18
  1.6 2.4 %collective-permute-start = (bf16[4,256,128]{2,1,0:T(8,128)(2,1)S(1)}, bf16[4,256,128]{2,1,0:T(8,128)(2,1)S(1)}, u32[]{:S(2)}, u32[]{:S(2)}) collective-permute-start(bf16[4,256,128]{2,1,0:T(8,128)(2,1)S(1)} %bitcast.16), channel_id=1, source_target_pairs={{0,1},{1,2},{2,3},{3,4},{4,5},{5,6},{6,7},{7,8},{8,9},{9,10},{10,1... | collective-permute-start | bytes 786440 | tf_op jit(solution)/shard_map/ppermute | solution.py:207
  4.0 10.1 %shard_map.85 = (bf16[8,256,256]{2,1,0:T(8,128)(2,1)}, bf16[2,256,128]{2,1,0:T(8,128)(2,1)}, f32[8,256,128]{2,1,0:T(8,128)}) custom-call(s32[4]{0:T(128)} %blocks_ref.3, s32[4]{0:T(128)} %tails_ref.3, bf16[8,256,256]{2,1,0:T(8,128)(2,1)} %bitcast.20, bf16[3,9,128,256]{3,2,1,0:T(8,128)(2,1)} %bitcast.18), custom_call_target="tpu_custom_call" | custom-call | flops 10000000000 | bytes 5000000 | tf_op jit(solution)/shard_map/pallas_call | solution.py:384
  14.1 1.3 %collective-permute-start.1 = (bf16[2,256,128]{2,1,0:T(8,128)(2,1)}, bf16[2,256,128]{2,1,0:T(8,128)(2,1)S(1)}, u32[]{:S(2)}, u32[]{:S(2)}) collective-permute-start(bf16[2,256,128]{2,1,0:T(8,128)(2,1)} %get-tuple-element.15), channel_id=1, source_target_pairs={{1,0},{2,1},{3,2},{4,3},{5,4},{6,5},{7,6},{8,7},{9,8},{10,9},{11,1... | collective-permute-start | bytes 393224 | tf_op jit(solution)/shard_map/ppermute | solution.py:207
  15.4 0.0 collective-permute-done.arrived_ref
  15.4 0.0 copy-start.1
  15.4 0.7 copy-done.1
  16.1 23.5 %shard_map.86 = (bf16[8,256,256]{2,1,0:T(8,128)(2,1)}, f32[8,256,128]{2,1,0:T(8,128)}, f32[3,1152,256]{2,1,0:T(8,128)}, bf16[12,256,128]{2,1,0:T(8,128)(2,1)}) custom-call(s32[4]{0:T(128)} %blocks_ref.3, s32[4]{0:T(128)} %tails_ref.3, bf16[4,256,128]{2,1,0:T(8,128)(2,1)} %copy-done.1, bf16[8,256,128]{2,1,0:T(8,128)(2,1)} %bitcast.17, ...), custom_call_target="tpu_custom_call" | custom-call | flops 12000000000 | bytes 12000000 | tf_op jit(solution)/shard_map/pallas_call | solution.py:402
  39.6 0.0 collective-permute-done.1.carried_ref
  39.6 0.0 copy-start
  39.6 0.6 copy-done
  40.2 62.0 %shard_map.87 = bf16[3,3584,128]{2,1,0:T(8,128)(2,1)} custom-call(bf16[12,256,128]{2,1,0:T(8,128)(2,1)} %get-tuple-element.12.ext_ref, f32[8,256,128]{2,1,0:T(8,128)} %get-tuple-element.13.pre_ref, f32[8,256,128]{2,1,0:T(8,128)} %get-tuple-element.14.tail_ref, bf16[2,256,128]{2,1,0:T(8,128)(2,1)} %copy-done, f32[3456,256]{1,0:T(8,128)} %bitcast.14), custom_call_target="tpu_custom_call" | custom-call | tf_op jit(solution)/shard_map/pallas_call | solution.py:182
  102.2 2.1 %slice_convert_fusion = f32[3,3456,128]{2,1,0:T(8,128)S(1)} fusion(bf16[3,3584,128]{2,1,0:T(8,128)(2,1)} %shard_map.87), kind=kLoop, calls=%fused_computation.1 | loop fusion | flops 1327104 | bytes 7962624 | tf_op jit(solution)/shard_map/convert_element_type | solution.py:200
  104.3 1.5 %fusion = (f32[1,3456,128]{2,1,0:T(8,128)S(1)}, f32[1,3456,128]{2,1,0:T(8,128)S(1)}, f32[1,3456,128]{2,1,0:T(8,128)}) fusion(f32[3,3456,128]{2,1,0:T(8,128)S(1)} %slice_convert_fusion), kind=kLoop, calls=%fused_computation.2 | loop fusion | bytes 10616832 | tf_op jit(solution)/shard_map/slice | solution.py:201
  105.9 2.1 %pad_maximum_fusion = f32[3,3,3,128,256]{4,3,2,1,0:T(8,128)} fusion(f32[3,3,3,128,128]{4,3,2,1,0:T(8,128)S(1)} %bitcast.13, f32[3,3,3,128,128]{4,3,2,1,0:T(8,128)S(1)} %bitcast.12), kind=kLoop, calls=%fused_computation | loop fusion | flops 884736 | bytes 7077888 | tf_op jit(solution)/shard_map/concatenate | solution.py:201
Async XLA Ops:
  1.6 13.8 %collective-permute-start = (bf16[4,256,128]{2,1,0:T(8,128)(2,1)S(1)}, bf16[4,256,128]{2,1,0:T(8,128)(2,1)S(1)}, u32[]{:S(2)}, u32[]{:S(2)}) collective-permute-start(bf16[4,256,128]{2,1,0:T(8,128)(2,1)S(1)} %bitcast.16), channel_id=1, source_target_pairs={{0,1},{1,2},{2,3},{3,4},{4,5},{5,6},{6,7},{7,8},{8,9},{9,10},{10,1... | collective-permute-start | bytes 786440 | tf_op jit(solution)/shard_map/ppermute | solution.py:207
  14.1 25.5 %collective-permute-start.1 = (bf16[2,256,128]{2,1,0:T(8,128)(2,1)}, bf16[2,256,128]{2,1,0:T(8,128)(2,1)S(1)}, u32[]{:S(2)}, u32[]{:S(2)}) collective-permute-start(bf16[2,256,128]{2,1,0:T(8,128)(2,1)} %get-tuple-element.15), channel_id=1, source_target_pairs={{1,0},{2,1},{3,2},{4,3},{5,4},{6,5},{7,6},{8,7},{9,8},{10,9},{11,1... | collective-permute-start | bytes 393224 | tf_op jit(solution)/shard_map/ppermute | solution.py:207
  15.4 0.7 copy-start.1
  39.6 0.7 copy-start

commit v3 on v0

--- a/solution.py
+++ b/solution.py
@@ -194,10 +194,20 @@
             )
 
 
-def back_kernel(width, scale, valid_ref, cot_ref, weight_ref, dout_ref, head_ref, tail_ref, taps, flipped, back):
+def clip_place(blocks_ref, tails_ref, count):
+    place = lax.axis_index("dp")
+    start, keep, valid = (jnp.int32(0), jnp.int32(1), jnp.int32(count))
+    for clip in range(blocks_ref.shape[0]):
+        keep = jnp.where(start == place, 0, keep)
+        start = start + blocks_ref[clip]
+        valid = jnp.where(start - 1 == place, tails_ref[clip], valid)
+    return keep, valid
+
+
+def back_kernel(width, scale, blocks_ref, tails_ref, cot_ref, weight_ref, dout_ref, head_ref, tail_ref, taps, flipped, back):
     count, pixels, channels = cot_ref.shape
     inner = tail_ref.shape[2]
-    valid = valid_ref[0]
+    keep, valid = clip_place(blocks_ref, tails_ref, count)
 
     @pl.loop(0, count)
     def _(f):
@@ -219,18 +229,37 @@
         for kt in range(3):
             back[pl.ds(f + kt, 2)] += part[:, :, kt * inner : (kt + 1) * inner]
 
-    head_ref[...] = back[:2].astype(jnp.bfloat16)
+    held = jnp.where(keep > 0, jnp.float32(1.0), jnp.float32(0.0))
+    head_ref[...] = (back[:2] * held).astype(jnp.bfloat16)
     tail_ref[...] = back[2:]
 
 
 def forward_kernel(
-    width, scalars_ref, ext_ref, one_ref, two_ref, dout_ref, feat_ref, pre_ref, grad_ref, taps, turned, pre, hidden
+    width,
+    blocks_ref,
+    tails_ref,
+    arrived_ref,
+    frames_ref,
+    one_ref,
+    two_ref,
+    dout_ref,
+    feat_ref,
+    pre_ref,
+    grad_ref,
+    ext_ref,
+    taps,
+    turned,
+    pre,
+    hidden,
 ):
     total, pixels, channels = ext_ref.shape
     count = total - 4
     inner = one_ref.shape[2]
     outer_channels = two_ref.shape[2]
-    keep, valid = (scalars_ref[0], scalars_ref[1])
+    keep, valid = clip_place(blocks_ref, tails_ref, count)
+    arrived = arrived_ref[...].astype(jnp.float32) * jnp.where(keep > 0, jnp.float32(1.0), jnp.float32(0.0))
+    ext_ref[:4] = arrived.astype(jnp.bfloat16)
+    ext_ref[4:] = frames_ref[...]
     spread(ext_ref, taps, width)
     pre[...] = jnp.zeros_like(pre)
 
@@ -305,18 +334,10 @@
     wide = weight_two.shape[-1]
     bf16, f32 = (jnp.bfloat16, jnp.float32)
     devices = lax.axis_size("dp")
-    place = lax.axis_index("dp")
     frames = frames.reshape(count, pixels, channels)
     cotangent = cotangent.reshape(count, pixels, wide)
     one = weight_one.reshape(3, 9 * channels, inner)
     arrived = from_behind(frames[count - 4 :], "dp", 1)
-    order = jnp.arange(clip_blocks.shape[0])
-    ends = jnp.sum(jnp.where(order[None, :] <= order[:, None], clip_blocks[None, :], 0), axis=1)
-    keep = jnp.where(jnp.any(ends - clip_blocks == place), 0, 1).astype(jnp.int32)
-    last_match = ends - 1 == place
-    tail_here = jnp.sum(jnp.where(last_match, tail_frames, 0))
-    valid = jnp.where(jnp.any(last_match), tail_here, count).astype(jnp.int32)
-    scalars = jnp.stack([keep, valid])
     scale = 1.0 / math.sqrt(devices * count * pixels)
 
     dout, head, tail = pl.pallas_call(
@@ -326,7 +347,7 @@
             jax.ShapeDtypeStruct((2, pixels, inner), bf16),
             jax.ShapeDtypeStruct((count, pixels, inner), f32),
         ),
-        in_specs=[SMEM, VMEM, VMEM],
+        in_specs=[SMEM, SMEM, VMEM, VMEM],
         out_specs=(VMEM, VMEM, VMEM),
         scratch_shapes=[
             pltpu.VMEM((count, pixels, 9 * wide), bf16),
@@ -335,18 +356,18 @@
         ],
         compiler_params=PARAMS,
         cost_estimate=pl.CostEstimate(flops=10**10, bytes_accessed=5 * 10**6, transcendentals=0),
-    )(scalars[1:], cotangent, weight_two.reshape(3, 9, inner, wide))
-    carried = from_behind(head * keep.astype(bf16), "dp", -1)
-    ext = jnp.concatenate([arrived * keep.astype(bf16), frames], axis=0)
-    features, pre, grad_two = pl.pallas_call(
+    )(clip_blocks, tail_frames, cotangent, weight_two.reshape(3, 9, inner, wide))
+    carried = from_behind(head, "dp", -1)
+    features, pre, grad_two, ext = pl.pallas_call(
         functools.partial(forward_kernel, width),
         out_shape=(
             jax.ShapeDtypeStruct((count, pixels, wide), bf16),
             jax.ShapeDtypeStruct((count, pixels, inner), f32),
             jax.ShapeDtypeStruct((3, 9 * inner, wide), f32),
+            jax.ShapeDtypeStruct((count + 4, pixels, channels), bf16),
         ),
-        in_specs=[SMEM, VMEM, VMEM, VMEM, VMEM],
-        out_specs=(VMEM, VMEM, VMEM),
+        in_specs=[SMEM, SMEM, VMEM, VMEM, VMEM, VMEM, VMEM],
+        out_specs=(VMEM, VMEM, VMEM, VMEM),
         scratch_shapes=[
             pltpu.VMEM((count + 4, pixels, 9 * max(channels, inner)), bf16),
             pltpu.VMEM((9 * inner, (count + 2) * pixels), bf16),
@@ -355,7 +376,7 @@
         ],
         compiler_params=PARAMS,
         cost_estimate=pl.CostEstimate(flops=12 * 10**9, bytes_accessed=12 * 10**6, transcendentals=0),
-    )(scalars, ext, one, weight_two.reshape(3, 9 * inner, wide), dout.reshape(count * pixels, wide))
+    )(clip_blocks, tail_frames, arrived, frames, one, weight_two.reshape(3, 9 * inner, wide), dout.reshape(count * pixels, wide))
     grad_one = pl.pallas_call(
         functools.partial(last_kernel, width),
         out_shape=jax.ShapeDtypeStruct((3, 9 * channels, inner), f32),

time: 114 us -> 107 us (0.939)
  other arithmetic: 8.35 us -> 2.42 us
  between operations: 2.66 us -> 0.69 us
    reduce_sum x2 -> x0, other arithmetic: 2.07 us -> none  [the longest x1 1.29 us: local(): tail_here = jnp.sum(jnp.where(last_match, tail_frames, 0))]
    reduce_or x1 -> x0, other arithmetic: 1.3 us -> none  [local(): jnp.any(ends - clip_blocks == place)]
  transfers between devices with their start and end apart: 2 -> 2, of which waited for: 0 -> 0; matrix products, arithmetic and copies ran while one was open for 5% -> 0% of each run, Pallas kernels for 29% -> 32%
where the time goes in v3:
time: 107 us; the launch traced here: 106 us
  Pallas kernels  94.2 us (88%)
  local copies, waits for them, and re-layouts  5.37 us (5%)
  starting transfers between devices  3.65 us (3%)
  other arithmetic  2.42 us (2%)
    pallas_call x1, Pallas kernels, sum_over_devices(): pl.pallas_call(functools.partial(sum_kernel, levels), out_shape=jax.Shape...  49.1 us
    pallas_call x1, Pallas kernels, local(): pl.pallas_call(functools.partial(forward_kernel, width), out_shape=(jax.S...  23.5 us
    pallas_call x1, Pallas kernels, local(): pl.pallas_call(functools.partial(last_kernel, width), out_shape=jax.Shape...  11.6 us
    pallas_call x1, Pallas kernels, local(): pl.pallas_call(functools.partial(back_kernel, width, scale), out_shape=(j...  10.1 us
    ppermute x2, starting transfers between devices, from_behind(): lax.ppermute(value, axis, [(source, source + steps) for source in range(i...  3.65 us
    unnamed x8, local copies, waits for them, and re-layouts  2.85 us
  transfers between devices with their start and end apart: 2, of which 0 were waited for; matrix products, arithmetic and copies ran while one was open for 0% of the time, Pallas kernels for 32%

profile of v3, /device:TPU:0, one launch (start us, length us, event | category | flops | bytes accessed | tf_op | source)
XLA Modules:
  0.0 106.4 jit_solution(17392212767074647073)
XLA Ops:
  0.6 1.0 slice.18
  1.6 2.4 %collective-permute-start = (bf16[4,256,128]{2,1,0:T(8,128)(2,1)S(1)}, bf16[4,256,128]{2,1,0:T(8,128)(2,1)S(1)}, u32[]{:S(2)}, u32[]{:S(2)}) collective-permute-start(bf16[4,256,128]{2,1,0:T(8,128)(2,1)S(1)} %bitcast.18), channel_id=1, source_target_pairs={{0,1},{1,2},{2,3},{3,4},{4,5},{5,6},{6,7},{7,8},{8,9},{9,10},{10,1... | collective-permute-start | bytes 786440 | tf_op jit(solution)/shard_map/ppermute | solution.py:149
  4.0 10.1 %shard_map.85 = (bf16[8,256,256]{2,1,0:T(8,128)(2,1)}, bf16[2,256,128]{2,1,0:T(8,128)(2,1)}, f32[8,256,128]{2,1,0:T(8,128)}) custom-call(s32[4]{0:T(128)} %blocks_ref.3, s32[4]{0:T(128)} %tails_ref.3, bf16[8,256,256]{2,1,0:T(8,128)(2,1)} %bitcast.22, bf16[3,9,128,256]{3,2,1,0:T(8,128)(2,1)} %bitcast.20), custom_call_target="tpu_custom_call" | custom-call | flops 10000000000 | bytes 5000000 | tf_op jit(solution)/shard_map/pallas_call | solution.py:343
  14.1 1.3 %collective-permute-start.1 = (bf16[2,256,128]{2,1,0:T(8,128)(2,1)}, bf16[2,256,128]{2,1,0:T(8,128)(2,1)S(1)}, u32[]{:S(2)}, u32[]{:S(2)}) collective-permute-start(bf16[2,256,128]{2,1,0:T(8,128)(2,1)} %get-tuple-element.15), channel_id=1, source_target_pairs={{1,0},{2,1},{3,2},{4,3},{5,4},{6,5},{7,6},{8,7},{9,8},{10,9},{11,1... | collective-permute-start | bytes 393224 | tf_op jit(solution)/shard_map/ppermute | solution.py:149
  15.4 0.0 collective-permute-done.arrived_ref
  15.4 0.0 copy-start.2
  15.4 0.7 copy-done.2
  16.1 23.5 %shard_map.86 = (bf16[8,256,256]{2,1,0:T(8,128)(2,1)}, f32[8,256,128]{2,1,0:T(8,128)}, f32[3,1152,256]{2,1,0:T(8,128)}, bf16[12,256,128]{2,1,0:T(8,128)(2,1)}) custom-call(s32[4]{0:T(128)} %blocks_ref.3, s32[4]{0:T(128)} %tails_ref.3, bf16[4,256,128]{2,1,0:T(8,128)(2,1)} %copy-done.2, bf16[8,256,128]{2,1,0:T(8,128)(2,1)} %bitcast.19, ...), custom_call_target="tpu_custom_call" | custom-call | flops 12000000000 | bytes 12000000 | tf_op jit(solution)/shard_map/pallas_call | solution.py:361
  39.6 0.0 collective-permute-done.1.carried_ref
  39.6 0.0 copy-start.3
  39.6 0.7 copy-done.3
  40.3 0.0 copy-start
  40.3 11.6 %shard_map.87 = f32[3,1152,128]{2,1,0:T(8,128)} custom-call(bf16[12,256,128]{2,1,0:T(8,128)(2,1)} %get-tuple-element.12.ext_ref, f32[8,256,128]{2,1,0:T(8,128)} %get-tuple-element.13.pre_ref, f32[8,256,128]{2,1,0:T(8,128)} %get-tuple-element.14.tail_ref, bf16[2,256,128]{2,1,0:T(8,128)(2,1)} %copy-done.3), custom_call_target="tpu_custom_call" | custom-call | flops 4000000000 | bytes 5000000 | tf_op jit(solution)/shard_map/pallas_call | solution.py:380
  51.8 0.0 copy-done
  51.8 0.0 copy-start.1
  51.8 1.5 %copy-done.1 = f32[3,1152,128]{2,1,0:T(8,128)S(1)} copy-done((f32[3,1152,128]{2,1,0:T(8,128)S(1)}, f32[3,1152,128]{2,1,0:T(8,128)}, u32[]{:S(2)}) %copy-start.1) | copy-done | bytes 1769496
  53.3 49.1 %shard_map.88 = bf16[3,3584,128]{2,1,0:T(8,128)(2,1)S(1)} custom-call(f32[3456,128]{1,0:T(8,128)S(1)} %bitcast.14, f32[3456,256]{1,0:T(8,128)S(1)} %bitcast.13), custom_call_target="tpu_custom_call" | custom-call | tf_op jit(solution)/shard_map/pallas_call | solution.py:123
  102.4 0.3 slice_convert_fusion
  102.8 1.5 %fusion = (f32[1,3456,128]{2,1,0:T(8,128)S(1)}, f32[1,3456,128]{2,1,0:T(8,128)S(1)}, f32[1,3456,128]{2,1,0:T(8,128)}) fusion(f32[3,3456,128]{2,1,0:T(8,128)S(1)} %slice_convert_fusion), kind=kLoop, calls=%fused_computation.2 | loop fusion | bytes 10616832 | tf_op jit(solution)/shard_map/slice | solution.py:140
  104.3 2.1 %pad_maximum_fusion = f32[3,3,3,128,256]{4,3,2,1,0:T(8,128)} fusion(f32[3,3,3,128,128]{4,3,2,1,0:T(8,128)S(1)} %bitcast.16, f32[3,3,3,128,128]{4,3,2,1,0:T(8,128)S(1)} %bitcast.15), kind=kLoop, calls=%fused_computation | loop fusion | flops 884736 | bytes 7077888 | tf_op jit(solution)/shard_map/concatenate | solution.py:142
Async XLA Ops:
  1.6 13.8 %collective-permute-start = (bf16[4,256,128]{2,1,0:T(8,128)(2,1)S(1)}, bf16[4,256,128]{2,1,0:T(8,128)(2,1)S(1)}, u32[]{:S(2)}, u32[]{:S(2)}) collective-permute-start(bf16[4,256,128]{2,1,0:T(8,128)(2,1)S(1)} %bitcast.18), channel_id=1, source_target_pairs={{0,1},{1,2},{2,3},{3,4},{4,5},{5,6},{6,7},{7,8},{8,9},{9,10},{10,1... | collective-permute-start | bytes 786440 | tf_op jit(solution)/shard_map/ppermute | solution.py:149
  14.1 25.5 %collective-permute-start.1 = (bf16[2,256,128]{2,1,0:T(8,128)(2,1)}, bf16[2,256,128]{2,1,0:T(8,128)(2,1)S(1)}, u32[]{:S(2)}, u32[]{:S(2)}) collective-permute-start(bf16[2,256,128]{2,1,0:T(8,128)(2,1)} %get-tuple-element.15), channel_id=1, source_target_pairs={{1,0},{2,1},{3,2},{4,3},{5,4},{6,5},{7,6},{8,7},{9,8},{10,9},{11,1... | collective-permute-start | bytes 393224 | tf_op jit(solution)/shard_map/ppermute | solution.py:149
  15.4 0.7 copy-start.2
  39.6 0.7 copy-start.3
  40.3 11.6 %copy-start = (f32[3,1152,256]{2,1,0:T(8,128)S(1)}, f32[3,1152,256]{2,1,0:T(8,128)}, u32[]{:S(2)}) copy-start(f32[3,1152,256]{2,1,0:T(8,128)} %get-tuple-element.16) | copy-start | bytes 10616836
  51.8 1.5 %copy-start.1 = (f32[3,1152,128]{2,1,0:T(8,128)S(1)}, f32[3,1152,128]{2,1,0:T(8,128)}, u32[]{:S(2)}) copy-start(f32[3,1152,128]{2,1,0:T(8,128)} %shard_map.87) | copy-start | bytes 5308420
